TPU v7x, 32 devices: a whole 2x2x4 slice. The times are simulated.
32 devices in a mesh: row: 8 (over z, x), col: 4 (over y, core).
Axes of the slice: x: 2, y: 2, z: 4, core: 2. Of those that a mesh axis runs over, the one named last changes fastest.
Arguments:
- features: bfloat16 [2048, 512], P(('row', 'col')), may hold values from -6 to 6
- tile_values: bfloat16 [8, 4, 64, 128, 128], P('row', 'col'), may hold values from -0.09375 to 0.09375
- tile_target: int32 [8, 4, 64], P('row', 'col'), may hold values from 0 to 1
- tile_anchor: int32 [8, 4, 64], P('row', 'col'), may hold values from 0 to 3
- live_tile_count: int32 [8, 4], P('row', 'col'), may hold values from 8 to 64, as said below
- mean_param: float32 [512, 512], P(None, 'col'), may hold values from -0.25 to 0.25
- spread_param: float32 [512, 512], P(None, 'col'), may hold values from -4.5 to -2.5
- noise_draws: bfloat16 [4, 512, 512], P(None, None, 'col'), may hold values from -6 to 6
- bias_shift: float32 [512], P('col'), may hold values from -3 to 3
- cotangent: bfloat16 [4, 2048, 512], P(None, 'row', 'col'), may hold values from -6 to 6
Outputs:
- activation: bfloat16 [4, 2048, 512], P(None, 'row', 'col')
- input_grad: bfloat16 [2048, 512], P(('row', 'col'))
- mean_grad: float32 [512, 512], P(None, 'col')
- spread_grad: float32 [512, 512], P(None, 'col')
- bias_grad: float32 [512], P('col')
Inputs may be any that keep to these rules, and one draw needn't show every extreme that they name: `live_tile_count`: some cell holds 64 live tiles in every draw.
All inputs are finite; a program needn't handle non-finite values.
Results may differ from a plain program's by a relative error of at most 0.02.
Values may be sent and summed in bfloat16 or wider, within the bound.
A program may use at most 64 MiB of HBM per device.

v0:
```python
import jax
import jax.numpy as jnp
from jax import lax
from jax.sharding import PartitionSpec as P


def tile_product(blocks, operand_tiles, pick_index, place_index, live_count, pattern, out_count):
    tile_size = blocks.shape[1]
    width = operand_tiles.shape[2]
    per_turn = 8
    turn_total = (live_count + per_turn - 1) // per_turn

    def one_turn(turn_index, running):
        first_slot = turn_index * per_turn
        block_part = lax.dynamic_slice_in_dim(blocks, first_slot, per_turn, 0)
        index_part = lax.dynamic_slice_in_dim(pick_index, first_slot, per_turn, 0)
        place_part = lax.dynamic_slice_in_dim(place_index, first_slot, per_turn, 0)
        slot_ids = first_slot + jnp.arange(per_turn, dtype=jnp.int32)
        live_part = (slot_ids < live_count).astype(jnp.float32)
        selected_tiles = jnp.take(operand_tiles, index_part, axis=0)
        tile_matmul_result = jnp.einsum(
            pattern, block_part, selected_tiles, preferred_element_type=jnp.float32
        )
        tile_matmul_result = tile_matmul_result * live_part[:, None, None]
        return running.at[place_part].add(tile_matmul_result)

    return lax.fori_loop(
        0, turn_total, one_turn, jnp.zeros((out_count, tile_size, width), jnp.float32)
    )


def shards(
    features,
    tile_values,
    tile_target,
    tile_anchor,
    live_tile_count,
    mean_param,
    spread_param,
    noise_draws,
    bias_shift,
    cotangent,
):
    node_rows = features.shape[0]
    width = features.shape[1]
    blocks = tile_values[0, 0]
    tile_size = blocks.shape[1]
    target_count = lax.axis_size("col") * node_rows // tile_size
    anchor_count = lax.axis_size("row") * node_rows // tile_size
    targets = tile_target[0, 0]
    anchors = tile_anchor[0, 0]
    live_count = live_tile_count[0, 0]
    gathered = lax.all_gather(features, "row", axis=0, tiled=True)
    source_tiles = gathered.reshape(anchor_count, tile_size, width)
    slab_part = tile_product(
        blocks, source_tiles, anchors, targets, live_count, "yuk,ykc->yuc", target_count
    )
    aggregate = lax.psum(slab_part.astype(jnp.bfloat16), "col").reshape(
        target_count * tile_size, width
    )
    weights = (
        mean_param[None] + jax.nn.softplus(spread_param)[None] * noise_draws.astype(jnp.float32)
    ).astype(jnp.bfloat16)
    preact = (
        jnp.einsum("nf,sfk->snk", aggregate, weights, preferred_element_type=jnp.float32)
        + bias_shift[None, None, :]
    )
    activation = jax.nn.silu(preact).astype(jnp.bfloat16)
    logistic = jax.nn.sigmoid(preact)
    pre_grad = (
        cotangent.astype(jnp.float32) * logistic * (1.0 + preact * (1.0 - logistic))
    ).astype(jnp.bfloat16)
    outer_sums = jnp.einsum("nf,snk->sfk", aggregate, pre_grad, preferred_element_type=jnp.float32)
    mean_part = jnp.sum(outer_sums, axis=0)
    spread_part = jnp.sum(noise_draws.astype(jnp.float32) * outer_sums, axis=0)
    bias_part = jnp.sum(pre_grad.astype(jnp.float32), axis=(0, 1))
    mean_grad, spread_total, bias_grad = (
        lax.psum(mean_part.astype(jnp.bfloat16), "row").astype(jnp.float32),
        lax.psum(spread_part.astype(jnp.bfloat16), "row").astype(jnp.float32),
        lax.psum(bias_part.astype(jnp.bfloat16), "row").astype(jnp.float32),
    )
    spread_grad = jax.nn.sigmoid(spread_param) * spread_total
    slab_terms = jnp.einsum("snk,sfk->nf", pre_grad, weights, preferred_element_type=jnp.float32)
    slab_grad = lax.psum(slab_terms.astype(jnp.bfloat16), "col")
    grad_tiles = slab_grad.reshape(target_count, tile_size, width)
    source_part = tile_product(
        blocks, grad_tiles, targets, anchors, live_count, "lwo,lwm->lom", anchor_count
    )
    input_grad = lax.psum_scatter(
        source_part.reshape(anchor_count * tile_size, width).astype(jnp.bfloat16),
        "row",
        scatter_dimension=0,
        tiled=True,
    )
    return (activation, input_grad, mean_grad, spread_grad, bias_grad)


def solution(mesh):
    placed = (
        P(("row", "col"), None),
        P("row", "col", None, None, None),
        P("row", "col", None),
        P("row", "col", None),
        P("row", "col"),
        P(None, "col"),
        P(None, "col"),
        P(None, None, "col"),
        P("col"),
        P(None, "row", "col"),
    )
    return jax.shard_map(
        shards,
        mesh=mesh,
        in_specs=placed,
        out_specs=(
            P(None, "row", "col"),
            P(("row", "col"), None),
            P(None, "col"),
            P(None, "col"),
            P("col"),
        ),
        check_vma=False,
    )
```

profile of v0, /device:TPU:0, one launch (start us, length us, event | category | flops | bytes accessed | tf_op | source)
XLA Modules:
  0.0 307.6 jit_solution(3518343962582917187)
XLA Ops:
  7.9 33.2 %all_gather.3 = bf16[512,512]{1,0:T(8,128)(2,1)S(1)} all-gather(bf16[64,512]{1,0:T(8,128)(2,1)} %param.14), channel_id=1, replica_groups=mesh['row'=8,'col'=4] {'row'}, dimensions={0}, use_global_device_ids=true | all-gather | bytes 589824 | tf_op jit(solution)/shard_map/all_gather | solution.py:53
  41.2 13.6 %while.20 = (s32[]{:T(128)}, f32[2,128,512]{2,1,0:T(8,128)S(1)}, s32[]{:T(128)}, s32[64]{0:T(128)}, bf16[64,128,128]{2,1,0:T(8,128)(2,1)}, /*index=5*/s32[64]{0:...) while((s32[]{:T(128)}, f32[2,128,512]{2,1,0:T(8,128)S(1)}, ...), condition=%wide.region_2.3_spmd, body=%wide.region_0.2_spmd.sunk | while | flops 135791712 | bytes 11802115 | solution.py:27
  41.2 1.4 compare_and_fusion.4
  42.6 1.6 gather_fusion
  44.2 1.8 convolution_multiply_fusion.4
  46.1 1.9 scatter_fusion
  48.0 1.4 compare_and_fusion.4
  49.4 1.6 gather_fusion
  51.0 1.8 convolution_multiply_fusion.4
  52.9 1.9 scatter_fusion
  54.8 0.7 convert_element_type.61
  55.6 4.2 %copy.27 = bf16[1,1,64,128,128]{3,4,2,1,0:T(8,128)(2,1)} copy(bf16[1,1,64,128,128]{4,3,2,1,0:T(8,128)(2,1)} %bitcast.31) | data formatting | bytes 4194304 | tf_op args[1]
  61.0 64.7 %all-reduce.5.cloned.1.call-done = bf16[256,512]{1,0:T(8,128)(2,1)} async-done(((bf16[256,512]{1,0:T(8,128)(2,1)}), bf16[256,512]{1,0:T(8,128)(2,1)}) %all-reduce.5.cloned.1.call-update) | async-done | bytes 262160 | tf_op jit(solution)/shard_map/psum | solution.py:58
  125.7 2.0 multiply_convert_fusion.1
  128.1 1.1 fusion.13
  129.2 1.0 fusion.16
  130.3 31.0 %all-reduce.7.cloned.1.call-done = bf16[2,128,512]{2,1,0:T(8,128)(2,1)} async-done(((bf16[2,128,512]{2,1,0:T(8,128)(2,1)}), bf16[2,128,512]{2,1,0:T(8,128)(2,1)}) %all-reduce.7.cloned.1.call-update) | async-done | bytes 262160 | tf_op jit(solution)/shard_map/psum | solution.py:84
  161.4 14.2 %while.21 = (s32[]{:T(128)}, f32[4,128,512]{2,1,0:T(8,128)S(1)}, s32[]{:T(128)}, s32[64]{0:T(128)S(1)}, bf16[64,128,128]{1,2,0:T(8,128)(2,1)}, /*index=5*/s32[64...) while((s32[]{:T(128)}, f32[4,128,512]{2,1,0:T(8,128)S(1)}, ...), condition=%wide.region_7.8_spmd, body=%wide.region_5.7_spmd.sunk | while | flops 135791712 | bytes 11801063 | solution.py:27
  162.2 2.6 gather_fusion.1
  164.7 1.8 convolution_multiply_fusion.5
  166.6 1.9 scatter_fusion.1
  169.2 2.6 gather_fusion.1
  171.8 1.8 convolution_multiply_fusion.5
  173.7 1.9 scatter_fusion.1
  175.6 0.8 convert_element_type.66
  176.6 28.5 %psum.39 = bf16[128]{0:T(256)(128)(2,1)S(1)} all-reduce(bf16[128]{0:T(256)(128)(2,1)S(1)} %get-tuple-element.159), channel_id=1, replica_groups=mesh['row'=8,'col'=4] {'row'}, use_global_device_ids=true, to_apply=%region_14.15 | all-reduce | flops 128 | bytes 512 | tf_op jit(solution)/shard_map/psum | solution.py:80
  205.6 0.8 copy.33
  206.5 29.2 %all-reduce.9.cloned.1.call-done = (bf16[512,128]{0,1:T(8,128)(2,1)}, bf16[512,128]{0,1:T(8,128)(2,1)}) async-done(((bf16[512,128]{0,1:T(8,128)(2,1)}, bf16[512,128]{0,1:T(8,128)(2,1)}), (bf16[512,128]{0,1:T(8,128)(2,1)}, bf16[512,128]{0,1:T(8,128)(2,1)})) %all-reduce.9.cloned.1.call-update) | async-done | bytes 262160 | tf_op jit(solution)/shard_map/psum | solution.py:78
  235.6 1.0 convert_multiply_fusion.2
  236.6 0.8 copy.35
  237.4 1.7 copy.34
  239.2 61.9 %reduce-scatter.2.cloned.1.call-done = bf16[64,512]{1,0:T(8,128)(2,1)} async-done(((bf16[512,512]{1,0:T(8,128)(2,1)}), bf16[64,512]{1,0:T(8,128)(2,1)}) %reduce-scatter.2.cloned.1.call-update) | async-done | bytes 65552 | tf_op jit(solution)/shard_map/reduce_scatter | solution.py:89
  (50 shorter events, 4.4 us)
Async XLA Ops:
  7.2 118.5 %all-reduce.5.cloned.1.call-start = ((), (), s32[]{:S(2)}) async-start(), calls=%async_computation.1 | async-start | bytes 524288 | tf_op jit(solution)/shard_map/psum | solution.py:58
  44.2 1.8 copy-start.5
  51.0 1.8 copy-start.5
  55.5 4.2 %copy-start.1 = (bf16[4,512,128]{2,1,0:T(8,128)(2,1)S(1)}, bf16[4,512,128]{2,1,0:T(8,128)(2,1)}, u32[]{:S(2)}) copy-start(bf16[4,512,128]{2,1,0:T(8,128)(2,1)} %param.21) | copy-start | bytes 1572868
  55.5 4.4 %copy-start = (f32[512,128]{1,0:T(8,128)S(1)}, f32[512,128]{1,0:T(8,128)}, u32[]{:S(2)}) copy-start(f32[512,128]{1,0:T(8,128)} %param.20) | copy-start | bytes 786436
  55.6 105.7 %all-reduce.7.cloned.1.call-start = ((), (), s32[]{:S(2)}) async-start(), calls=%async_computation.2 | async-start | bytes 524288 | tf_op jit(solution)/shard_map/psum | solution.py:84
  59.8 0.9 copy-start.2
  59.8 1.1 copy-start.3
  59.8 65.9 %copy-start.9 = (f32[128]{0:T(128)S(1)}, f32[128]{0:T(128)}, u32[]{:S(2)}) copy-start(f32[128]{0:T(128)} %param.22) | copy-start | bytes 1540
  127.7 1.5 copy-start.8
  128.0 33.3 %copy-start.6 = (s32[64]{0:T(128)S(1)}, s32[64]{0:T(128)}, u32[]{:S(2)}) copy-start(s32[64]{0:T(128)} %get-tuple-element.370) | copy-start | bytes 772
  128.0 33.3 %copy-start.7 = (s32[64]{0:T(128)S(1)}, s32[64]{0:T(128)}, u32[]{:S(2)}) copy-start(s32[64]{0:T(128)} %get-tuple-element.371) | copy-start | bytes 772
  129.1 106.5 %all-reduce.9.cloned.1.call-start = ((), (), s32[]{:S(2)}) async-start(), calls=%async_computation.4 | async-start | bytes 524288 | tf_op jit(solution)/shard_map/psum | solution.py:78
  130.3 170.8 %reduce-scatter.2.cloned.1.call-start = ((), (), s32[]{:S(2)}) async-start(), calls=%async_computation.3 | async-start | bytes 589824 | tf_op jit(solution)/shard_map/reduce_scatter | solution.py:89
  175.6 30.0 %copy-start.4 = (bf16[4,256,128]{1,2,0:T(8,128)(2,1)S(1)}, bf16[4,256,128]{1,2,0:T(8,128)(2,1)}, u32[]{:S(2)}) copy-start(bf16[4,256,128]{1,2,0:T(8,128)(2,1)} %get-tuple-element.163) | copy-start | bytes 786436
Sparse Core Ops, SparseCore 0:
  55.6 70.0 all-reduce.4
  129.3 31.9 all-reduce.6
  164.7 70.8 all-reduce.8
  239.8 61.2 reduce-scatter.1
where the time goes:
time: 307 us; the launch traced here: 308 us
  waiting for transfers between devices  187 us (61%)
  blocking collectives  61.7 us (20%)
  local copies, waits for them, and re-layouts  17.2 us (6%)
  other arithmetic  15.6 us (5%)
  between operations  14.6 us (5%)
  matrix products  11.4 us (4%)
    psum x1, waiting for transfers between devices, shards(): lax.psum(slab_part.astype(jnp.bfloat16), 'col')  64.7 us
    reduce_scatter x1, waiting for transfers between devices, shards(): lax.psum_scatter(source_part.reshape(anchor_count * tile_size, width).ast...  61.9 us
    all_gather x1, blocking collectives, shards(): gathered = lax.all_gather(features, 'row', axis=0, tiled=True)  33.2 us
    psum x1, waiting for transfers between devices, shards(): slab_grad = lax.psum(slab_terms.astype(jnp.bfloat16), 'col')  31 us
    psum x1, waiting for transfers between devices, shards(): lax.psum(mean_part.astype(jnp.bfloat16), 'row').astype(jnp.float32)  29.2 us
    psum x1, blocking collectives, shards(): lax.psum(bias_part.astype(jnp.bfloat16), 'row').astype(jnp.float32)  28.5 us
    unnamed x26, local copies, waits for them, and re-layouts  8.61 us
    gather x4, local copies, waits for them, and re-layouts, one_turn(): selected_tiles = jnp.take(operand_tiles, index_part, axis=0)  8.29 us
  transfers between devices with their start and end apart: 4, of which 4 were waited for; matrix products, arithmetic and copies ran while one was open for 8% of the time, Pallas kernels for 0%

commit v1 on v0

v1 whole, which is shorter than its diff:
```python
import functools

import jax
import jax.numpy as jnp
from jax import lax
from jax.experimental import pallas as pl
from jax.experimental.pallas import tpu as pltpu
from jax.sharding import PartitionSpec as P

MESH = pl.DeviceIdType.MESH
PIECES = 2
BF = jnp.bfloat16
F32 = jnp.float32


def kernel(
    n_row, n_col,
    feat, tiles, target, anchor, live, mean, spread, noise, bias, cot,
    act_o, input_o, mean_o, spread_o, bias_o,
    tiles_v, mean_v, spread_v, noise_v, cot_v, act_v,
    xg, adj, adj_t, wcat, pgcat, agg, slab,
    c_out, c_in, c_own, c_half, c_y,
    b_out, b_own, b_in, b_sum, b_z,
    w_part, w_in, w_all, bias_part, bias_in,
    load_sem, act_sem, gz_s, gz_r, gx_s, gx_r,
    c1_s, c1_r, cy_s, cy_r, c3_s, c3_r,
    bx_s, bx_r, bz_s, bz_r, w1_s, w1_r, w2_s, w2_r, bi_s, bi_r,
):
    nodes, width = feat.shape
    slots, tile, _ = tiles.shape
    samples, _, panel = noise.shape
    rows = nodes * n_col
    half = rows // 2
    piece = half // PIECES
    zn, yn = n_row // 2, n_col // 2
    targets = rows // tile
    anchors = n_row * nodes // tile
    r, c = lax.axis_index("row"), lax.axis_index("col")
    z, x = r // 2, r % 2
    y, core = c // 2, c % 2
    r_twin = z * 2 + 1 - x
    c_twin = y * 2 + 1 - core
    pending = []

    def at(index, size):
        return pl.ds(pl.multiple_of(index * size, size), size)

    def send(src, dst, s_sem, r_sem, row, col):
        copy = pltpu.make_async_remote_copy(
            src_ref=src, dst_ref=dst, send_sem=s_sem, recv_sem=r_sem,
            device_id=(row, col), device_id_type=MESH,
        )
        copy.start()
        pending.append(copy)
        return copy

    loads = []
    pairs = ((spread, spread_v), (mean, mean_v), (noise, noise_v), (tiles, tiles_v), (cot, cot_v),
             (feat, xg.at[at(r, nodes)]))
    for i, (src, dst) in enumerate(pairs):
        load = pltpu.make_async_copy(src, dst, load_sem.at[i])
        load.start()
        loads.append(load)

    barrier = pltpu.get_barrier_semaphore()
    for k in range(1, n_row):
        pl.semaphore_signal(barrier, inc=1, device_id=((r + k) % n_row, c), device_id_type=MESH)
    for k in range(1, n_col):
        pl.semaphore_signal(barrier, inc=1, device_id=(r, (c + k) % n_col), device_id_type=MESH)
    pl.semaphore_wait(barrier, n_row + n_col - 2)

    here = xg.at[at(r, nodes)]
    along_z = {}
    order = sorted(range(1, zn), key=lambda k: min(k, zn - k))
    for k in order[::-1]:
        along_z[k] = send(feat, here, gz_s.at[k], gz_r.at[k], ((z + k) % zn) * 2 + x, c)
    along_x = [send(feat, here, gx_s.at[0], gx_r.at[0], r_twin, c)]

    def forward(k):
        along_z[k].wait_recv()
        spot = xg.at[at(((z - k + zn) % zn) * 2 + x, nodes)]
        along_x.append(send(spot, spot, gx_s.at[k], gx_r.at[k], r_twin, c))

    def make_weights():
        for load in loads[:3]:
            load.wait()
        soft = jnp.log1p(jnp.exp(spread_v[...]))
        for s in range(samples):
            wcat[:, s * panel:(s + 1) * panel] = (
                mean_v[...] + soft * noise_v[s].astype(F32)
            ).astype(BF)

    def make_adjacency(first, last):
        @pl.loop(first, last)
        def _(b):
            tb, ab = b // anchors, b % anchors

            def step(t, total):
                hit = (t < live[0]) & (target[t] == tb) & (anchor[t] == ab)
                return total + jnp.where(hit, 1.0, 0.0).astype(F32) * tiles_v[t].astype(F32)

            total = lax.fori_loop(0, slots, step, jnp.zeros((tile, tile), F32), unroll=8)
            adj[at(tb, tile), at(ab, tile)] = total.astype(BF)
            turned = total.T.astype(BF)
            adj_t[0, at(ab, nodes), at(tb, tile)] = turned[:nodes]
            adj_t[1, at(ab, nodes), at(tb, tile)] = turned[nodes:]

    blocks = targets * anchors
    make_weights()
    loads[3].wait()
    done = 0
    for i, k in enumerate(order):
        upto = blocks * (i + 1) // len(order)
        make_adjacency(done, upto)
        done = upto
        forward(k)
    loads[5].wait()
    for copy in along_x:
        copy.wait_recv()

    def col_reduce(i, term, full, between, own_done):
        first, crossing, last = [], [], []
        for q in range(PIECES):
            c_out[i, q] = term((1 - core) * PIECES + q).astype(BF)
            first.append(send(c_out.at[i, q], c_in.at[i, q], c1_s.at[i, q], c1_r.at[i, q], r, c_twin))
        for q in range(PIECES):
            c_own[q] = term(core * PIECES + q)
        for q in range(PIECES):
            first[q].wait_recv()
            c_half[i, q] = (c_own[q] + c_in[i, q].astype(F32)).astype(BF)
            for k in range(1, yn):
                crossing.append(send(
                    c_half.at[i, q], c_y.at[i, k, q], cy_s.at[i, k, q], cy_r.at[i, k, q],
                    r, ((y + k) % yn) * 2 + core,
                ))
        between()
        for q in range(PIECES):
            total = c_half[i, q].astype(F32)
            for k in range(1, yn):
                crossing[q * (yn - 1) + k - 1].wait_recv()
                total += c_y[i, k, q].astype(F32)
            spot = at(core * PIECES + q, piece)
            full[spot, :] = total.astype(BF)
            last.append(send(full.at[spot], full.at[spot], c3_s.at[i, q], c3_r.at[i, q], r, c_twin))
        own_done()
        for copy in last:
            copy.wait_recv()

    def neurons(which):
        spot = at(which, half)
        pre_all = jnp.dot(agg[spot, :], wcat[...], preferred_element_type=F32)
        for s in range(samples):
            pre = pre_all[:, s * panel:(s + 1) * panel] + bias[...]
            sig = jax.nn.sigmoid(pre)
            act_v[s, spot, :] = (pre * sig).astype(BF)
            pgcat[spot, s * panel:(s + 1) * panel] = (
                cot_v[s, spot, :].astype(F32) * sig * (1.0 + pre * (1.0 - sig))
            ).astype(BF)

    def own_neurons():
        loads[4].wait()
        neurons(core)

    col_reduce(
        0, lambda q: jnp.dot(adj[at(q, piece), :], xg[...], preferred_element_type=F32),
        agg, lambda: None, own_neurons,
    )
    neurons(1 - core)
    act_copy = pltpu.make_async_copy(act_v, act_o, act_sem.at[0])
    act_copy.start()

    share = width // n_row
    w_first, w_last, bias_sent = [], [], []

    def weight_terms():
        step = 256
        for f in range(0, width, step):
            outer = lax.dot_general(
                agg[:, f:f + step], pgcat[...], (((0,), (0,)), ((), ())), preferred_element_type=F32
            )
            parts = [outer[:, s * panel:(s + 1) * panel] for s in range(samples)]
            w_part[0, f:f + step, :] = sum(parts[1:], parts[0]).astype(BF)
            scaled = [noise_v[s, f:f + step, :].astype(F32) * parts[s] for s in range(samples)]
            w_part[1, f:f + step, :] = sum(scaled[1:], scaled[0]).astype(BF)
        sums = jnp.sum(pgcat[...].astype(F32), axis=0, keepdims=True)
        sums = [sums[:, s * panel:(s + 1) * panel] for s in range(samples)]
        bias_part[...] = jnp.broadcast_to(sum(sums[1:], sums[0]), bias_part.shape)
        for k in range(1, n_row):
            to = (r + k) % n_row
            w_first.append(send(w_part.at[:, at(to, share)], w_in.at[k], w1_s.at[k], w1_r.at[k], to, c))
            bias_sent.append(send(bias_part, bias_in.at[k], bi_s.at[k], bi_r.at[k], to, c))

    col_reduce(
        1,
        lambda q: lax.dot_general(
            pgcat[at(q, piece), :], wcat[...], (((1,), (1,)), ((), ())), preferred_element_type=F32
        ),
        slab, weight_terms, lambda: None,
    )

    b_out[...] = jnp.dot(adj_t[1 - x], slab[...], preferred_element_type=F32).astype(BF)
    b_first = {}
    for k in [*order[::-1], 0]:
        b_first[k] = send(b_out.at[at((z + k) % zn, nodes)], b_in.at[k], bx_s.at[k], bx_r.at[k], r_twin, c)
    b_own[...] = jnp.dot(adj_t[x], slab[...], preferred_element_type=F32)

    b_last = {}
    for k in order[::-1]:
        to = (z + k) % zn
        b_first[k].wait_recv()
        b_sum[k] = (b_own[at(to, nodes), :] + b_in[k].astype(F32)).astype(BF)
        b_last[k] = send(b_sum.at[k], b_z.at[k], bz_s.at[k], bz_r.at[k], to * 2 + x, c)

    total = w_part[:, at(r, share), :].astype(F32)
    for k in range(1, n_row):
        w_first[k - 1].wait_recv()
        total += w_in[k].astype(F32)
    spot = w_all.at[:, at(r, share)]
    w_all[:, at(r, share), :] = total.astype(BF)
    for k in range(1, n_row):
        w_last.append(send(spot, spot, w2_s.at[k], w2_r.at[k], (r + k) % n_row, c))

    total = bias_part[...]
    for k in range(1, n_row):
        bias_sent[k - 1].wait_recv()
        total += bias_in[k]
    bias_o[...] = total[:1]

    b_first[0].wait_recv()
    total = b_own[at(z, nodes), :] + b_in[0].astype(F32)
    for k in order:
        b_last[k].wait_recv()
        total += b_z[k].astype(F32)
    input_o[...] = total.astype(BF)

    for copy in w_last:
        copy.wait_recv()
    mean_o[...] = w_all[0].astype(F32)
    spread_o[...] = jax.nn.sigmoid(spread_v[...]) * w_all[1].astype(F32)
    act_copy.wait()
    for copy in pending:
        copy.wait_send()


def shards(
    n_row, n_col, features, tile_values, tile_target, tile_anchor, live_tile_count,
    mean_param, spread_param, noise_draws, bias_shift, cotangent,
):
    nodes, width = features.shape
    samples, _, panel = noise_draws.shape
    slots, tile = tile_values.shape[2:4]
    rows = nodes * n_col
    half = rows // 2
    piece = half // PIECES
    zn, yn = n_row // 2, n_col // 2
    share = width // n_row
    group = n_row * nodes
    any_space = pl.BlockSpec(memory_space=pl.ANY)
    smem = pl.BlockSpec(memory_space=pltpu.SMEM)
    vmem = pl.BlockSpec(memory_space=pltpu.VMEM)
    dma = pltpu.SemaphoreType.DMA
    buf = pltpu.VMEM
    scratch = [
        buf((slots, tile, tile), BF), buf((width, panel), F32), buf((width, panel), F32),
        buf((samples, width, panel), BF), buf((samples, rows, panel), BF), buf((samples, rows, panel), BF),
        buf((group, width), BF), buf((rows, group), BF), buf((2, group // 2, rows), BF),
        buf((width, samples * panel), BF), buf((rows, samples * panel), BF),
        buf((rows, width), BF), buf((rows, width), BF),
        buf((2, PIECES, piece, width), BF), buf((2, PIECES, piece, width), BF),
        buf((PIECES, piece, width), F32), buf((2, PIECES, piece, width), BF),
        buf((2, yn, PIECES, piece, width), BF),
        buf((group // 2, width), BF), buf((group // 2, width), F32), buf((zn, nodes, width), BF),
        buf((zn, nodes, width), BF), buf((zn, nodes, width), BF),
        buf((2, width, panel), BF), buf((n_row, 2, share, panel), BF), buf((2, width, panel), BF),
        buf((8, panel), F32), buf((n_row, 8, panel), F32),
        dma((6,)), dma((1,)), dma((zn,)), dma((zn,)), dma((zn,)), dma((zn,)),
        dma((2, PIECES)), dma((2, PIECES)), dma((2, yn, PIECES)), dma((2, yn, PIECES)),
        dma((2, PIECES)), dma((2, PIECES)),
        dma((zn,)), dma((zn,)), dma((zn,)), dma((zn,)),
        dma((n_row,)), dma((n_row,)), dma((n_row,)), dma((n_row,)), dma((n_row,)), dma((n_row,)),
    ]
    act, input_grad, mean_grad, spread_grad, bias_grad = pl.pallas_call(
        functools.partial(kernel, n_row, n_col),
        out_shape=(
            jax.ShapeDtypeStruct((samples, rows, panel), BF),
            jax.ShapeDtypeStruct((nodes, width), BF),
            jax.ShapeDtypeStruct((width, panel), F32),
            jax.ShapeDtypeStruct((width, panel), F32),
            jax.ShapeDtypeStruct((1, panel), F32),
        ),
        in_specs=[any_space, any_space, smem, smem, smem, any_space, any_space, any_space, vmem, any_space],
        out_specs=(any_space, vmem, vmem, vmem, vmem),
        scratch_shapes=scratch,
        compiler_params=pltpu.CompilerParams(
            collective_id=0, has_side_effects=True, vmem_limit_bytes=56 * 1024 * 1024
        ),
    )(
        features, tile_values[0, 0], tile_target[0, 0], tile_anchor[0, 0], live_tile_count[0],
        mean_param, spread_param, noise_draws, bias_shift[None], cotangent,
    )
    return act, input_grad, mean_grad, spread_grad, bias_grad[0]


def solution(mesh):
    placed = (
        P(("row", "col"), None),
        P("row", "col", None, None, None),
        P("row", "col", None),
        P("row", "col", None),
        P("row", "col"),
        P(None, "col"),
        P(None, "col"),
        P(None, None, "col"),
        P("col"),
        P(None, "row", "col"),
    )
    return jax.shard_map(
        functools.partial(shards, mesh.shape["row"], mesh.shape["col"]),
        mesh=mesh,
        in_specs=placed,
        out_specs=(
            P(None, "row", "col"),
            P(("row", "col"), None),
            P(None, "col"),
            P(None, "col"),
            P("col"),
        ),
        check_vma=False,
    )
```

time: 307 us -> 59.9 us (0.20)
  waiting for transfers between devices: 187 us -> 0 us
  blocking collectives: 61.7 us -> 0 us
  Pallas kernels: 0 us -> 50.6 us
  other arithmetic: 15.6 us -> 0 us
  between operations: 14.6 us -> 1.29 us
  matrix products: 11.4 us -> 0 us
  local copies, waits for them, and re-layouts: 17.2 us -> 7.65 us
    psum x3 -> x0, waiting for transfers between devices: 125 us -> none  [the longest x1 64.7 us: shards(): lax.psum(slab_part.astype(jnp.bfloat16), 'col')]
    reduce_scatter x1 -> x0, waiting for transfers between devices: 61.9 us -> none  [shards(): lax.psum_scatter(source_part.reshape(anchor_count * tile_size, width).ast...]
    pallas_call x0 -> x1, Pallas kernels: none -> 50.6 us  [shards(): pl.pallas_call(functools.partial(kernel, n_row, n_col), out_shape=(jax.Sh...]
    all_gather x1 -> x0, blocking collectives: 33.2 us -> none  [shards(): gathered = lax.all_gather(features, 'row', axis=0, tiled=True)]
    psum x1 -> x0, blocking collectives: 28.5 us -> none  [shards(): lax.psum(bias_part.astype(jnp.bfloat16), 'row').astype(jnp.float32)]
    dot_general x7 -> x0, matrix products: 11.4 us -> none  [the longest x4 7.23 us: one_turn(): jnp.einsum(pattern, block_part, selected_tiles, preferred_element_type=jn...]
    gather x4 -> x0, local copies, waits for them, and re-layouts: 8.29 us -> none  [one_turn(): selected_tiles = jnp.take(operand_tiles, index_part, axis=0)]
    scatter-add x4 -> x0, other arithmetic: 7.51 us -> none  [one_turn(): return running.at[place_part].add(tile_matmul_result)]
  transfers between devices with their start and end apart: 4 -> 0, of which waited for: 4 -> 0; matrix products, arithmetic and copies ran while one was open for 8% -> 0% of each run, Pallas kernels for 0% -> 0%
where the time goes in v1:
time: 59.9 us; the launch traced here: 59.5 us
  Pallas kernels  50.6 us (84%)
  local copies, waits for them, and re-layouts  7.65 us (13%)
  between operations  1.29 us (2%)
    pallas_call x1, Pallas kernels, shards(): pl.pallas_call(functools.partial(kernel, n_row, n_col), out_shape=(jax.Sh...  50.6 us
    unnamed x5, local copies, waits for them, and re-layouts  7.65 us

profile of v1, /device:TPU:0, one launch (start us, length us, event | category | flops | bytes accessed | tf_op | source)
XLA Modules:
  0.0 59.5 jit_solution(14054846317013439683)
XLA Ops:
  1.3 50.6 %shard_map.137 = (bf16[4,256,128]{2,1,0:T(8,128)(2,1)}, bf16[64,512]{1,0:T(8,128)(2,1)}, f32[512,128]{1,0:T(8,128)}, f32[512,128]{1,0:T(8,128)}, f32[1,128]{1,0:T(1,128)}) custom-call(bf16[64,512]{1,0:T(8,128)(2,1)} %feat.1, bf16[64,128,128]{2,1,0:T(8,128)(2,1)} %bitcast.7, s32[64]{0:T(128)} %bitcast.8, s32[64]{0:T(128)} %bitcast.9, s32[1]{0:T(128)} %bitcast.6.live, ...), custom_call_target="tpu_custom_call" | custom-call | tf_op jit(solution)/shard_map/pallas_call | solution.py:282
  51.9 1.7 %copy.21 = bf16[4,256,128]{2,1,0:T(8,128)(2,1)} copy(bf16[4,256,128]{2,1,0:T(8,128)(2,1)} %get-tuple-element.20) | data formatting | bytes 524288
  53.5 1.5 %copy.22 = bf16[64,512]{1,0:T(8,128)(2,1)} copy(bf16[64,512]{1,0:T(8,128)(2,1)} %get-tuple-element.21) | data formatting | bytes 131072
  55.0 1.7 %copy.23 = f32[512,128]{1,0:T(8,128)} copy(f32[512,128]{1,0:T(8,128)} %get-tuple-element.22) | data formatting | bytes 524288
  56.7 1.7 %copy.24 = f32[512,128]{1,0:T(8,128)} copy(f32[512,128]{1,0:T(8,128)} %get-tuple-element.23) | data formatting | bytes 524288
  58.3 1.2 %copy.25 = f32[128]{0:T(128)} copy(f32[128]{0:T(128)} %bitcast.11) | data formatting | bytes 1024

commit v2 on v1

--- a/solution.py
+++ b/solution.py
@@ -9,6 +9,7 @@
 
 MESH = pl.DeviceIdType.MESH
 PIECES = 2
+HALVES = 2
 BF = jnp.bfloat16
 F32 = jnp.float32
 
@@ -16,15 +17,15 @@
 def kernel(
     n_row, n_col,
     feat, tiles, target, anchor, live, mean, spread, noise, bias, cot,
-    act_o, input_o, mean_o, spread_o, bias_o,
+    act_o, input_o, grads_o, bias_o,
     tiles_v, mean_v, spread_v, noise_v, cot_v, act_v,
     xg, adj, adj_t, wcat, pgcat, agg, slab,
     c_out, c_in, c_own, c_half, c_y,
     b_out, b_own, b_in, b_sum, b_z,
     w_part, w_in, w_all, bias_part, bias_in,
-    load_sem, act_sem, gz_s, gz_r, gx_s, gx_r,
+    load_sem, act_sem, gz_s, gz_r, gx_s, gx_r, gp_s, gp_r,
     c1_s, c1_r, cy_s, cy_r, c3_s, c3_r,
-    bx_s, bx_r, bz_s, bz_r, w1_s, w1_r, w2_s, w2_r, bi_s, bi_r,
+    bx_s, bx_r, bz_s, bz_r, w1_s, w1_r, wz_s, wz_r, wx_s, wx_r, bi_s, bi_r,
 ):
     nodes, width = feat.shape
     slots, tile, _ = tiles.shape
@@ -69,17 +70,45 @@
         pl.semaphore_signal(barrier, inc=1, device_id=(r, (c + k) % n_col), device_id_type=MESH)
     pl.semaphore_wait(barrier, n_row + n_col - 2)
 
+    pairs_z = zn // 2
+    z_pair = z + 1 - 2 * (z % 2)
+    across = range(1, zn - 1)
+    part = nodes // HALVES
+
+    def to_z(i):
+        if i == 0:
+            return z
+        if i == zn - 1:
+            return z_pair
+        return ((z // 2 + (i + 1) // 2) % pairs_z) * 2 + (z % 2 + (i - 1) % 2) % 2
+
+    def from_z(i):
+        if i in (0, zn - 1):
+            return to_z(i)
+        return ((z // 2 - (i + 1) // 2 + pairs_z) % pairs_z) * 2 + (z % 2 + (i - 1) % 2) % 2
+
     here = xg.at[at(r, nodes)]
-    along_z = {}
-    order = sorted(range(1, zn), key=lambda k: min(k, zn - k))
-    for k in order[::-1]:
-        along_z[k] = send(feat, here, gz_s.at[k], gz_r.at[k], ((z + k) % zn) * 2 + x, c)
-    along_x = [send(feat, here, gx_s.at[0], gx_r.at[0], r_twin, c)]
-
-    def forward(k):
-        along_z[k].wait_recv()
-        spot = xg.at[at(((z - k + zn) % zn) * 2 + x, nodes)]
-        along_x.append(send(spot, spot, gx_s.at[k], gx_r.at[k], r_twin, c))
+    along_z, along_x = {}, []
+
+    def cross(h):
+        for i in across:
+            along_z[i, h] = send(
+                feat.at[pl.ds(h * part, part)], xg.at[at(r * HALVES + h, part)],
+                gz_s.at[i, h], gz_r.at[i, h], to_z(i) * 2 + x, c,
+            )
+
+    cross(0)
+    along_x.append(send(feat, here, gx_s.at[0, 0], gx_r.at[0, 0], r_twin, c))
+    along_x.append(send(feat, here, gp_s.at[0], gp_r.at[0], z_pair * 2 + x, c))
+    along_x.append(send(feat, here, gp_s.at[1], gp_r.at[1], z_pair * 2 + 1 - x, c))
+    for h in range(1, HALVES):
+        cross(h)
+
+    def forward(h):
+        for i in across:
+            along_z[i, h].wait_recv()
+            spot = xg.at[at((from_z(i) * 2 + x) * HALVES + h, part)]
+            along_x.append(send(spot, spot, gx_s.at[i, h], gx_r.at[i, h], r_twin, c))
 
     def make_weights():
         for load in loads[:3]:
@@ -96,7 +125,7 @@
             tb, ab = b // anchors, b % anchors
 
             def step(t, total):
-                hit = (t < live[0]) & (target[t] == tb) & (anchor[t] == ab)
+                hit = (t < live[0, 0]) & (target[t] == tb) & (anchor[t] == ab)
                 return total + jnp.where(hit, 1.0, 0.0).astype(F32) * tiles_v[t].astype(F32)
 
             total = lax.fori_loop(0, slots, step, jnp.zeros((tile, tile), F32), unroll=8)
@@ -109,11 +138,11 @@
     make_weights()
     loads[3].wait()
     done = 0
-    for i, k in enumerate(order):
-        upto = blocks * (i + 1) // len(order)
+    for h in range(HALVES):
+        upto = blocks * (h + 1) // HALVES
         make_adjacency(done, upto)
         done = upto
-        forward(k)
+        forward(h)
     loads[5].wait()
     for copy in along_x:
         copy.wait_recv()
@@ -199,26 +228,37 @@
     )
 
     b_out[...] = jnp.dot(adj_t[1 - x], slab[...], preferred_element_type=F32).astype(BF)
-    b_first = {}
-    for k in [*order[::-1], 0]:
-        b_first[k] = send(b_out.at[at((z + k) % zn, nodes)], b_in.at[k], bx_s.at[k], bx_r.at[k], r_twin, c)
+    b_first, b_last = {}, {}
+    queue = [(i, h) for h in range(HALVES) for i in across]
+    queue += [(i, h) for i in (zn - 1, 0) for h in range(HALVES)]
+    for i, h in queue:
+        b_first[i, h] = send(
+            b_out.at[at(to_z(i) * HALVES + h, part)], b_in.at[i, h], bx_s.at[i, h], bx_r.at[i, h], r_twin, c
+        )
     b_own[...] = jnp.dot(adj_t[x], slab[...], preferred_element_type=F32)
 
-    b_last = {}
-    for k in order[::-1]:
-        to = (z + k) % zn
-        b_first[k].wait_recv()
-        b_sum[k] = (b_own[at(to, nodes), :] + b_in[k].astype(F32)).astype(BF)
-        b_last[k] = send(b_sum.at[k], b_z.at[k], bz_s.at[k], bz_r.at[k], to * 2 + x, c)
+    def onward(i, h):
+        b_first[i, h].wait_recv()
+        b_sum[i, h] = (b_own[at(to_z(i) * HALVES + h, part), :] + b_in[i, h].astype(F32)).astype(BF)
+        b_last[i, h] = send(b_sum.at[i, h], b_z.at[i, h], bz_s.at[i, h], bz_r.at[i, h], to_z(i) * 2 + x, c)
+
+    for i, h in queue[:-2 * HALVES]:
+        onward(i, h)
 
     total = w_part[:, at(r, share), :].astype(F32)
     for k in range(1, n_row):
         w_first[k - 1].wait_recv()
         total += w_in[k].astype(F32)
     spot = w_all.at[:, at(r, share)]
-    w_all[:, at(r, share), :] = total.astype(BF)
-    for k in range(1, n_row):
-        w_last.append(send(spot, spot, w2_s.at[k], w2_r.at[k], (r + k) % n_row, c))
+    w_all[0, at(r, share), :] = total[0].astype(BF)
+    w_all[1, at(r, share), :] = (jax.nn.sigmoid(spread_v[at(r, share), :]) * total[1]).astype(BF)
+    w_z = {}
+    for i in range(1, zn):
+        w_z[i] = send(spot, spot, wz_s.at[i], wz_r.at[i], to_z(i) * 2 + x, c)
+    w_last.append(send(spot, spot, wx_s.at[0], wx_r.at[0], r_twin, c))
+
+    for h in range(HALVES):
+        onward(zn - 1, h)
 
     total = bias_part[...]
     for k in range(1, n_row):
@@ -226,20 +266,39 @@
         total += bias_in[k]
     bias_o[...] = total[:1]
 
-    b_first[0].wait_recv()
-    total = b_own[at(z, nodes), :] + b_in[0].astype(F32)
-    for k in order:
-        b_last[k].wait_recv()
-        total += b_z[k].astype(F32)
-    input_o[...] = total.astype(BF)
+    for i in [zn - 1, *across]:
+        w_z[i].wait_recv()
+        spot = w_all.at[:, at(from_z(i) * 2 + x, share)]
+        w_last.append(send(spot, spot, wx_s.at[i], wx_r.at[i], r_twin, c))
+
+    for h in range(HALVES):
+        b_first[0, h].wait_recv()
+        total = b_own[at(z * HALVES + h, part), :] + b_in[0, h].astype(F32)
+        for i in range(1, zn):
+            b_last[i, h].wait_recv()
+            total += b_z[i, h].astype(F32)
+        input_o[h * part:(h + 1) * part, :] = total.astype(BF)
 
     for copy in w_last:
         copy.wait_recv()
-    mean_o[...] = w_all[0].astype(F32)
-    spread_o[...] = jax.nn.sigmoid(spread_v[...]) * w_all[1].astype(F32)
+    grads_o[...] = w_all[...]
     act_copy.wait()
     for copy in pending:
         copy.wait_send()
+
+
+def finish(act, input_grad, grads, bias, act_o, input_o, mean_o, spread_o, bias_o, sem):
+    copies = [
+        pltpu.make_async_copy(act, act_o, sem.at[0]),
+        pltpu.make_async_copy(input_grad, input_o, sem.at[1]),
+    ]
+    for copy in copies:
+        copy.start()
+    mean_o[...] = grads[0].astype(F32)
+    spread_o[...] = grads[1].astype(F32)
+    bias_o[...] = bias[...]
+    for copy in copies:
+        copy.wait()
 
 
 def shards(
@@ -269,18 +328,35 @@
         buf((2, PIECES, piece, width), BF), buf((2, PIECES, piece, width), BF),
         buf((PIECES, piece, width), F32), buf((2, PIECES, piece, width), BF),
         buf((2, yn, PIECES, piece, width), BF),
-        buf((group // 2, width), BF), buf((group // 2, width), F32), buf((zn, nodes, width), BF),
-        buf((zn, nodes, width), BF), buf((zn, nodes, width), BF),
+        buf((group // 2, width), BF), buf((group // 2, width), F32), buf((zn, HALVES, nodes // HALVES, width), BF),
+        buf((zn, HALVES, nodes // HALVES, width), BF), buf((zn, HALVES, nodes // HALVES, width), BF),
         buf((2, width, panel), BF), buf((n_row, 2, share, panel), BF), buf((2, width, panel), BF),
         buf((8, panel), F32), buf((n_row, 8, panel), F32),
-        dma((6,)), dma((1,)), dma((zn,)), dma((zn,)), dma((zn,)), dma((zn,)),
+        dma((6,)), dma((1,)), *[dma((zn, HALVES))] * 4, dma((2,)), dma((2,)),
         dma((2, PIECES)), dma((2, PIECES)), dma((2, yn, PIECES)), dma((2, yn, PIECES)),
         dma((2, PIECES)), dma((2, PIECES)),
-        dma((zn,)), dma((zn,)), dma((zn,)), dma((zn,)),
-        dma((n_row,)), dma((n_row,)), dma((n_row,)), dma((n_row,)), dma((n_row,)), dma((n_row,)),
+        *[dma((zn, HALVES))] * 4, dma((n_row,)), dma((n_row,)), *[dma((zn,))] * 4, dma((n_row,)), dma((n_row,)),
     ]
+    held = pl.pallas_call(
+        functools.partial(kernel, n_row, n_col),
+        out_shape=(
+            jax.ShapeDtypeStruct((samples, rows, panel), BF),
+            jax.ShapeDtypeStruct((nodes, width), BF),
+            jax.ShapeDtypeStruct((2, width, panel), BF),
+            jax.ShapeDtypeStruct((1, panel), F32),
+        ),
+        in_specs=[any_space, any_space, smem, smem, smem, any_space, any_space, any_space, vmem, any_space],
+        out_specs=(any_space, vmem, vmem, vmem),
+        scratch_shapes=scratch,
+        compiler_params=pltpu.CompilerParams(
+            collective_id=0, has_side_effects=True, vmem_limit_bytes=56 * 1024 * 1024
+        ),
+    )(
+        features, tile_values[0, 0], tile_target[0, 0], tile_anchor[0, 0], live_tile_count,
+        mean_param, spread_param, noise_draws, bias_shift[None], cotangent,
+    )
     act, input_grad, mean_grad, spread_grad, bias_grad = pl.pallas_call(
-        functools.partial(kernel, n_row, n_col),
+        finish,
         out_shape=(
             jax.ShapeDtypeStruct((samples, rows, panel), BF),
             jax.ShapeDtypeStruct((nodes, width), BF),
@@ -288,16 +364,10 @@
             jax.ShapeDtypeStruct((width, panel), F32),
             jax.ShapeDtypeStruct((1, panel), F32),
         ),
-        in_specs=[any_space, any_space, smem, smem, smem, any_space, any_space, any_space, vmem, any_space],
-        out_specs=(any_space, vmem, vmem, vmem, vmem),
-        scratch_shapes=scratch,
-        compiler_params=pltpu.CompilerParams(
-            collective_id=0, has_side_effects=True, vmem_limit_bytes=56 * 1024 * 1024
-        ),
-    )(
-        features, tile_values[0, 0], tile_target[0, 0], tile_anchor[0, 0], live_tile_count[0],
-        mean_param, spread_param, noise_draws, bias_shift[None], cotangent,
-    )
+        in_specs=[any_space, any_space, vmem, vmem],
+        out_specs=(any_space, any_space, vmem, vmem, vmem),
+        scratch_shapes=[dma((2,))],
+    )(*held)
     return act, input_grad, mean_grad, spread_grad, bias_grad[0]
 
 

time: 59.9 us -> 64.6 us (1.078)
  Pallas kernels: 50.6 us -> 63.2 us
  local copies, waits for them, and re-layouts: 7.65 us -> 0 us
    pallas_call x0 -> x1, Pallas kernels: none -> 12.8 us  [shards(): pl.pallas_call(finish, out_shape=(jax.ShapeDtypeStruct((samples, rows, pa...]
    unnamed x5 -> x0, local copies, waits for them, and re-layouts: 7.65 us -> none
where the time goes in v2:
time: 64.6 us; the launch traced here: 64.5 us
  Pallas kernels  63.2 us (98%)
  between operations  1.29 us (2%)
    pallas_call x1, Pallas kernels, shards(): pl.pallas_call(functools.partial(kernel, n_row, n_col), out_shape=(jax.Sh...  50.4 us
    pallas_call x1, Pallas kernels, shards(): pl.pallas_call(finish, out_shape=(jax.ShapeDtypeStruct((samples, rows, pa...  12.8 us

profile of v2, /device:TPU:0, one launch (start us, length us, event | category | flops | bytes accessed | tf_op | source)
XLA Modules:
  0.0 64.5 jit_solution(9772576761487298015)
XLA Ops:
  1.3 50.4 %shard_map.137 = (bf16[4,256,128]{2,1,0:T(8,128)(2,1)}, bf16[64,512]{1,0:T(8,128)(2,1)}, bf16[2,512,128]{2,1,0:T(8,128)(2,1)}, f32[1,128]{1,0:T(1,128)}) custom-call(bf16[64,512]{1,0:T(8,128)(2,1)} %feat.1, bf16[64,128,128]{2,1,0:T(8,128)(2,1)} %bitcast.5, s32[64]{0:T(128)} %bitcast.6, s32[64]{0:T(128)} %bitcast.7, s32[1,1]{1,0:T(1,128)S(6)} %copy.15.live, ...), custom_call_target="tpu_custom_call" | custom-call | tf_op jit(solution)/shard_map/pallas_call | solution.py:340
  51.7 12.8 %shard_map.138 = (bf16[4,256,128]{2,1,0:T(8,128)(2,1)}, bf16[64,512]{1,0:T(8,128)(2,1)}, f32[512,128]{1,0:T(8,128)}, f32[512,128]{1,0:T(8,128)}, f32[1,128]{1,0:T(1,128)}) custom-call(bf16[4,256,128]{2,1,0:T(8,128)(2,1)} %get-tuple-element.14.act, bf16[64,512]{1,0:T(8,128)(2,1)} %get-tuple-element.15.input_grad, ...), custom_call_target="tpu_custom_call" | custom-call | tf_op jit(solution)/shard_map/pallas_call | solution.py:358

commit v3 on v2

--- a/solution.py
+++ b/solution.py
@@ -287,18 +287,12 @@
         copy.wait_send()
 
 
-def finish(act, input_grad, grads, bias, act_o, input_o, mean_o, spread_o, bias_o, sem):
-    copies = [
-        pltpu.make_async_copy(act, act_o, sem.at[0]),
-        pltpu.make_async_copy(input_grad, input_o, sem.at[1]),
-    ]
-    for copy in copies:
-        copy.start()
+def finish(act, input_grad, grads, bias, act_o, input_o, mean_o, spread_o, bias_o):
+    act_o[...] = act[...]
+    input_o[...] = input_grad[...]
     mean_o[...] = grads[0].astype(F32)
     spread_o[...] = grads[1].astype(F32)
     bias_o[...] = bias[...]
-    for copy in copies:
-        copy.wait()
 
 
 def shards(
@@ -364,9 +358,9 @@
             jax.ShapeDtypeStruct((width, panel), F32),
             jax.ShapeDtypeStruct((1, panel), F32),
         ),
-        in_specs=[any_space, any_space, vmem, vmem],
-        out_specs=(any_space, any_space, vmem, vmem, vmem),
-        scratch_shapes=[dma((2,))],
+        in_specs=[vmem] * 4,
+        out_specs=(vmem,) * 5,
+        compiler_params=pltpu.CompilerParams(vmem_limit_bytes=32 * 1024 * 1024),
     )(*held)
     return act, input_grad, mean_grad, spread_grad, bias_grad[0]
 

time: 64.6 us -> 56.3 us (0.87)
  Pallas kernels: 63.2 us -> 51.4 us
  local copies, waits for them, and re-layouts: 0 us -> 3.36 us
    pallas_call x1, Pallas kernels: 12.8 us -> 0.95 us  [shards(): pl.pallas_call(finish, out_shape=(jax.ShapeDtypeStruct((samples, rows, pa...]
    unnamed x0 -> x8, local copies, waits for them, and re-layouts: none -> 3.36 us
where the time goes in v3:
time: 56.3 us; the launch traced here: 56 us
  Pallas kernels  51.4 us (91%)
  local copies, waits for them, and re-layouts  3.36 us (6%)
  between operations  1.3 us (2%)
    pallas_call x1, Pallas kernels, shards(): pl.pallas_call(functools.partial(kernel, n_row, n_col), out_shape=(jax.Sh...  50.4 us
    unnamed x8, local copies, waits for them, and re-layouts  3.36 us

profile of v3, /device:TPU:0, one launch (start us, length us, event | category | flops | bytes accessed | tf_op | source)
XLA Modules:
  0.0 56.0 jit_solution(16639773442709099066)
XLA Ops:
  1.3 50.4 %shard_map.137 = (bf16[4,256,128]{2,1,0:T(8,128)(2,1)}, bf16[64,512]{1,0:T(8,128)(2,1)}, bf16[2,512,128]{2,1,0:T(8,128)(2,1)}, f32[1,128]{1,0:T(1,128)}) custom-call(bf16[64,512]{1,0:T(8,128)(2,1)} %feat.1, bf16[64,128,128]{2,1,0:T(8,128)(2,1)} %bitcast.5, s32[64]{0:T(128)} %bitcast.6, s32[64]{0:T(128)} %bitcast.7, s32[1,1]{1,0:T(1,128)S(6)} %copy.15.live, ...), custom_call_target="tpu_custom_call" | custom-call | tf_op jit(solution)/shard_map/pallas_call | solution.py:334
  51.7 0.0 copy-start
  51.7 0.9 %copy-done = bf16[4,256,128]{2,1,0:T(8,128)(2,1)S(1)} copy-done((bf16[4,256,128]{2,1,0:T(8,128)(2,1)S(1)}, bf16[4,256,128]{2,1,0:T(8,128)(2,1)}, u32[]{:S(2)}) %copy-start) | copy-done | bytes 262168
  52.7 0.0 copy-start.1
  52.7 0.9 %copy-done.1 = bf16[2,512,128]{2,1,0:T(8,128)(2,1)S(1)} copy-done((bf16[2,512,128]{2,1,0:T(8,128)(2,1)S(1)}, bf16[2,512,128]{2,1,0:T(8,128)(2,1)}, u32[]{:S(2)}) %copy-start.1) | copy-done | bytes 262168
  53.6 0.0 copy-start.2
  53.6 0.8 %copy-done.2 = bf16[64,512]{1,0:T(8,128)(2,1)S(1)} copy-done((bf16[64,512]{1,0:T(8,128)(2,1)S(1)}, bf16[64,512]{1,0:T(8,128)(2,1)}, u32[]{:S(2)}) %copy-start.2) | copy-done | bytes 65560
  54.4 0.0 copy-start.3
  54.4 0.6 %copy-done.3 = f32[1,128]{1,0:T(1,128)S(1)} copy-done((f32[1,128]{1,0:T(1,128)S(1)}, f32[1,128]{1,0:T(1,128)}, u32[]{:S(2)}) %copy-start.3) | copy-done | bytes 536
  55.1 1.0 %shard_map.138 = (bf16[4,256,128]{2,1,0:T(8,128)(2,1)}, bf16[64,512]{1,0:T(8,128)(2,1)}, f32[512,128]{1,0:T(8,128)}, f32[512,128]{1,0:T(8,128)}, f32[1,128]{1,0:T(1,128)}) custom-call(bf16[4,256,128]{2,1,0:T(8,128)(2,1)S(1)} %copy-done, bf16[64,512]{1,0:T(8,128)(2,1)S(1)} %copy-done.2, bf16[2,512,128]{2,1,0:T(8,128)(2,1)S(1)} %copy-done.1, ...), custom_call_target="tpu_custom_call" | custom-call | tf_op jit(solution)/shard_map/pallas_call | solution.py:352
Async XLA Ops:
  51.7 1.0 %copy-start = (bf16[4,256,128]{2,1,0:T(8,128)(2,1)S(1)}, bf16[4,256,128]{2,1,0:T(8,128)(2,1)}, u32[]{:S(2)}) copy-start(bf16[4,256,128]{2,1,0:T(8,128)(2,1)} %get-tuple-element.14.act) | copy-start | bytes 786436
  52.7 0.9 %copy-start.1 = (bf16[2,512,128]{2,1,0:T(8,128)(2,1)S(1)}, bf16[2,512,128]{2,1,0:T(8,128)(2,1)}, u32[]{:S(2)}) copy-start(bf16[2,512,128]{2,1,0:T(8,128)(2,1)} %get-tuple-element.16.grads) | copy-start | bytes 786436
  53.6 0.8 %copy-start.2 = (bf16[64,512]{1,0:T(8,128)(2,1)S(1)}, bf16[64,512]{1,0:T(8,128)(2,1)}, u32[]{:S(2)}) copy-start(bf16[64,512]{1,0:T(8,128)(2,1)} %get-tuple-element.15.input_grad) | copy-start | bytes 196612
  54.4 0.6 %copy-start.3 = (f32[1,128]{1,0:T(1,128)S(1)}, f32[1,128]{1,0:T(1,128)}, u32[]{:S(2)}) copy-start(f32[1,128]{1,0:T(1,128)} %get-tuple-element.17.bias) | copy-start | bytes 1540
